TPU v7x, 32 devices: a whole 2x2x4 slice. The times are simulated.
32 devices in a mesh: groups: 2 (over x), expert: 8 (over z, y), dp: 2 (over core).
Axes of the slice: x: 2, y: 2, z: 4, core: 2. Of those that a mesh axis runs over, the one named last changes fastest.
Arguments:
- output_grad: bfloat16 [2048, 4096], P(('groups', 'expert', 'dp')), parts along dimension 0, may hold values from -6 to 6
- route_weights: float32 [2048, 2], P(('groups', 'expert', 'dp')), parts along dimension 0, may hold values from 0.2 to 1
- routes: int32 [2048, 2], P(('groups', 'expert', 'dp')), parts along dimension 0, may hold values from 0 to 7, as said below
- route_slots: int32 [2048, 2], P(('groups', 'expert', 'dp')), parts along dimension 0, may hold values from 0 to 11, as said below
- counts: int32 [32, 2], P(('groups', 'expert', 'dp')), parts along dimension 0, may hold values from 1 to 12, as said below
- saved_gate: bfloat16 [4, 96, 16384], P(('groups', 'dp'), None, 'expert'), parts along dimension 0, may hold values from -6 to 6
- saved_up: bfloat16 [4, 96, 16384], P(('groups', 'dp'), None, 'expert'), parts along dimension 0, may hold values from -6 to 6
- gate_weight: bfloat16 [4096, 16384], P(None, 'expert'), may hold values from -0.09375 to 0.09375
- up_weight: bfloat16 [4096, 16384], P(None, 'expert'), may hold values from -0.09375 to 0.09375
- down_weight: bfloat16 [16384, 4096], P('expert'), may hold values from -0.0625 to 0.0625
Outputs:
- token_grad: bfloat16 [2048, 4096], P(('groups', 'expert', 'dp')), parts along dimension 0
- down_grad: float32 [32768, 4096], P(('groups', 'expert', 'dp')), parts along dimension 0
There are 2 independent parts, one for each index of `groups`. A program takes and returns all parts, laid end to end along the dimension named above; an argument that names none is the same for every part. Nothing has to cross between parts.
Inputs may be any that keep to these rules, and one draw needn't show every extreme that they name: `routes`: each token names two different experts; for each owner and each expert x below 2, exactly counts[owner, x] of the owner's tokens name x. `route_slots`: where a token names an expert x below 2, its slot is below counts[owner, x], and the owner's tokens that name x hold distinct slots. Row o counts the tokens of owner o that name each expert below 2.
All inputs are finite; a program needn't handle non-finite values.
Results may differ from a plain program's by a relative error of at most 0.0064.
Values may be sent and summed in bfloat16 or wider, within the bound.
A program may use at most 256 MiB of HBM per device.

v0:
```python
import jax
import jax.numpy as jnp
from jax import lax
from jax.sharding import PartitionSpec as P

EXP_WIN = 2


def local(
    output_grad,
    route_weights,
    routes,
    route_slots,
    counts,
    saved_gate,
    saved_up,
    gate_weight,
    up_weight,
    down_weight,
):
    senders = lax.axis_size("expert")
    shards = senders // EXP_WIN
    capacity = saved_gate.shape[1] // senders
    tokens = output_grad.shape[0]
    width = output_grad.shape[1]
    places = jnp.arange(capacity, dtype=jnp.int32)
    experts = jnp.arange(EXP_WIN, dtype=jnp.int32)
    matches = (routes[:, :, None, None] == experts[None, None, :, None]) & (
        route_slots[:, :, None, None] == places[None, None, None, :]
    )
    live = places[None, :] < counts[0][:, None]
    scaled = (route_weights[:, :, None] * output_grad[:, None, :].astype(jnp.float32)).astype(
        jnp.bfloat16
    )
    placing = (matches & live[None, None, :, :]).astype(jnp.bfloat16)
    packed = jnp.einsum(
        "tkxc,tkd->xcd", placing, scaled, preferred_element_type=jnp.float32
    ).astype(jnp.bfloat16)
    outgoing = jnp.repeat(packed, shards, axis=0)
    arrived = lax.all_to_all(outgoing, "expert", split_axis=0, concat_axis=0, tiled=True)
    expert_rows = arrived.reshape(senders * capacity, width)
    gate_values = saved_gate[0].astype(jnp.float32)
    up_values = saved_up[0].astype(jnp.float32)
    contract_last = (((1,), (1,)), ((), ()))
    upstream = lax.dot_general(
        expert_rows, down_weight, contract_last, preferred_element_type=jnp.float32
    )
    sigmoid_gate = jax.nn.sigmoid(gate_values)
    grad_up = (upstream * gate_values * sigmoid_gate).astype(jnp.bfloat16)
    grad_gate = (
        upstream * up_values * sigmoid_gate * (1.0 + gate_values * (1.0 - sigmoid_gate))
    ).astype(jnp.bfloat16)
    hidden = (gate_values * sigmoid_gate * up_values).astype(jnp.bfloat16)
    stacked_grad = jnp.concatenate([grad_gate, grad_up], axis=1)
    stacked_weight = jnp.concatenate([gate_weight, up_weight], axis=1)
    partial_value = lax.dot_general(
        stacked_grad, stacked_weight, contract_last, preferred_element_type=jnp.float32
    ).astype(jnp.bfloat16)
    combine_table = jnp.sum(matches.astype(jnp.float32), axis=1).reshape(tokens, EXP_WIN * capacity)
    received = lax.all_to_all(
        partial_value.reshape(senders, capacity, width),
        "expert",
        split_axis=0,
        concat_axis=0,
        tiled=True,
    )
    columns = received.shape[2]
    summed = jnp.sum(
        received.reshape(EXP_WIN, shards, capacity, columns), axis=1, dtype=jnp.float32
    )
    gathered = jnp.dot(
        combine_table,
        summed.reshape(EXP_WIN * capacity, columns),
        precision=lax.Precision.HIGHEST,
        preferred_element_type=jnp.float32,
    )
    token_grad = gathered.astype(jnp.bfloat16)
    contract_first = (((0,), (0,)), ((), ()))
    columns = hidden
    down_grad = lax.psum_scatter(
        lax.dot_general(columns, expert_rows, contract_first, preferred_element_type=jnp.float32),
        "dp",
        scatter_dimension=0,
        tiled=True,
    )
    return (token_grad, down_grad)


def solution(mesh):
    placed = (
        P(("groups", "expert", "dp"), None),
        P(("groups", "expert", "dp"), None),
        P(("groups", "expert", "dp"), None),
        P(("groups", "expert", "dp"), None),
        P(("groups", "expert", "dp"), None),
        P(("groups", "dp"), None, "expert"),
        P(("groups", "dp"), None, "expert"),
        P(None, "expert"),
        P(None, "expert"),
        P("expert", None),
    )
    return jax.shard_map(
        local,
        mesh=mesh,
        in_specs=placed,
        out_specs=(P(("groups", "expert", "dp"), None), P(("groups", "expert", "dp"), None)),
        check_vma=False,
    )
```

profile of v0, /device:TPU:0, one launch (start us, length us, event | category | flops | bytes accessed | tf_op | source)
XLA Modules:
  0.0 132.6 jit_solution(15527430340704899184)
XLA Ops:
  7.2 0.0 reduce-scatter.2.cloned.1.call-start
  7.2 0.7 iota_compare_fusion.2
  7.9 0.7 iota_compare_fusion.1
  8.6 0.7 iota_compare_fusion
  9.3 1.1 convert_element_type.57
  10.4 1.1 fusion.8
  11.5 0.1 broadcast_in_dim.2
  11.6 32.8 %all_to_all.10 = bf16[8,12,4096]{2,1,0:T(8,128)(2,1)S(1)} all-to-all(bf16[8,12,4096]{2,1,0:T(8,128)(2,1)S(1)} %bitcast.61), channel_id=1, replica_groups=mesh['groups'=2,'expert'=8,'dp'=2] {'expert'}, dimensions={0} | all-to-all | bytes 1572864 | tf_op jit(solution)/shard_map/all_to_all | solution.py:40
  44.5 0.2 reshape.63
  44.6 14.3 %fusion.33 = f32[2048,4096]{1,0:T(8,128)} fusion(bf16[96,4096]{1,0:T(8,128)(2,1)S(1)} %reshape.63, bf16[1,96,2048]{2,1,0:T(8,128)(2,1)} %param.16, bf16[1,96,2048]{2,1,0:T(8,128)(2,1)} %param.15), kind=kOutput, calls=%fused_computation.39 | convolution fusion | flops 1612185600 | bytes 35127296 | tf_op jit(solution)/shard_map/dot_general | solution.py:81
  58.9 0.0 copy-start
  58.9 0.0 copy-start.1
  58.9 0.0 reduce-scatter.2.cloned.1.call-update
  58.9 1.0 copy-done
  59.9 0.1 copy-done.1
  60.0 11.9 %fusion.19 = (bf16[96,2048]{1,0:T(8,128)(2,1)S(1)}, bf16[96,2048]{1,0:T(8,128)(2,1)S(1)}) fusion(bf16[1,96,2048]{2,1,0:T(8,128)(2,1)S(1)} %copy-done, bf16[1,96,2048]{2,1,0:T(8,128)(2,1)S(1)} %copy-done.1, bf16[96,4096]{1,0:T(8,128)(2,1)S(1)} %reshape.63, bf16[2048,4096]{1,0:T(8,128)(2,1)} %param.19), kind=kOutput, calls=%fused_computation.25 | convolution fusion | flops 1613561856 | bytes 19136512 | tf_op jit(solution)/shard_map/dot_general | solution.py:45
  71.9 22.2 %fusion.4 = bf16[96,4096]{1,0:T(8,128)(2,1)S(1)} fusion(bf16[4096,2048]{1,0:T(8,128)(2,1)} %param.18, bf16[4096,2048]{1,0:T(8,128)(2,1)} %param.17, bf16[96,2048]{1,0:T(8,128)(2,1)S(1)} %get-tuple-element.3, bf16[96,2048]{1,0:T(8,128)(2,1)S(1)} %get-tuple-element.2), kind=kOutput, calls=%fused_computation.4 | convolution fusion | flops 3290300416 | bytes 35127296 | tf_op jit(solution)/shard_map/dot_general | solution.py:56
  94.1 1.2 reshape.64
  95.2 3.6 %all-to-all-start.1 = ((bf16[8,12,4096]{2,1,0:T(8,128)(2,1)}), bf16[8,12,4096]{2,1,0:T(8,128)(2,1)S(1)}, u32[]{:S(2)}, u32[]{:S(2)}) async-start(bf16[8,12,4096]{2,1,0:T(8,128)(2,1)} %reshape.64), calls=%async_computation.1 | async-start | bytes 2097152 | tf_op jit(solution)/shard_map/all_to_all | solution.py:60
  98.9 24.8 %all-to-all-done.1 = bf16[8,12,4096]{2,1,0:T(8,128)(2,1)S(1)} async-done(((bf16[8,12,4096]{2,1,0:T(8,128)(2,1)}), bf16[8,12,4096]{2,1,0:T(8,128)(2,1)S(1)}, u32[]{:S(2)}, u32[]{:S(2)}) %all-to-all-start.1) | async-done | bytes 786464 | tf_op jit(solution)/shard_map/all_to_all | solution.py:60
  123.7 0.2 convert_reduce_fusion
  123.9 1.8 %fusion.7 = bf16[64,4096]{1,0:T(8,128)(2,1)} fusion(f32[64,2,12]{0,2,1:T(8,128)S(1)} %fusion.36, f32[2,12,4096]{2,1,0:T(8,128)S(1)} %convert_reduce_fusion), kind=kOutput, calls=%fused_computation.6 | convolution fusion | flops 75759616 | bytes 923648 | tf_op jit(solution)/shard_map/dot_general | solution.py:71
  125.7 0.0 reduce-scatter.2.cloned.1.call-done
  (1 shorter events, 0.0 us)
Async XLA Ops:
  7.2 118.6 %reduce-scatter.2.cloned.1.call-start = ((), (), s32[]{:S(2)}) async-start(), calls=%async_computation.3 | async-start | bytes 50331648 | tf_op jit(solution)/shard_map/reduce_scatter | solution.py:80
  58.9 1.0 copy-start
  58.9 1.1 copy-start.1
  95.2 28.5 %all-to-all-start.1 = ((bf16[8,12,4096]{2,1,0:T(8,128)(2,1)}), bf16[8,12,4096]{2,1,0:T(8,128)(2,1)S(1)}, u32[]{:S(2)}, u32[]{:S(2)}) async-start(bf16[8,12,4096]{2,1,0:T(8,128)(2,1)} %reshape.64), calls=%async_computation.1 | async-start | bytes 2097152 | tf_op jit(solution)/shard_map/all_to_all | solution.py:60
Sparse Core Ops, SparseCore 0:
  59.0 44.2 reduce-scatter.1
where the time goes:
time: 133 us
  matrix products  51.2 us (38%)
  blocking collectives  32.8 us (25%)
  waiting for transfers between devices  24.8 us (19%)
  between operations  14.1 us (11%)
  starting transfers between devices  3.68 us (3%)
  other arithmetic  3.41 us (3%)
  local copies, waits for them, and re-layouts  2.53 us (2%)
    all_to_all x1, blocking collectives, local(): lax.all_to_all(outgoing, 'expert', split_axis=0, concat_axis=0, tiled=True)  32.8 us
    all_to_all x1, waiting for transfers between devices, local(): lax.all_to_all(partial_value.reshape(senders, capacity, width), 'expert',...  24.8 us
    dot_general x1, matrix products, local(): lax.dot_general(stacked_grad, stacked_weight, contract_last, preferred_el...  22.2 us
    dot_general x1, matrix products, local(): lax.dot_general(columns, expert_rows, contract_first, preferred_element_t...  14.3 us
    dot_general x1, matrix products, local(): lax.dot_general(expert_rows, down_weight, contract_last, preferred_elemen...  11.9 us
    all_to_all x1, starting transfers between devices, local(): lax.all_to_all(partial_value.reshape(senders, capacity, width), 'expert',...  3.65 us
  transfers between devices with their start and end apart: 2, of which 1 were waited for; matrix products, arithmetic and copies ran while one was open for 28% of the time, Pallas kernels for 0%

commit v1 on v0

v1 whole, which is shorter than its diff:
```python
import functools

import jax
import jax.numpy as jnp
from jax import lax
from jax.experimental import pallas as pl
from jax.experimental.pallas import tpu as pltpu
from jax.sharding import PartitionSpec as P

EXP_WIN = 2
QUAD = 4
PAD = 16
CHUNKS = 4
MESH = pl.DeviceIdType.MESH
F32 = jnp.float32
BF16 = jnp.bfloat16
NT = (((1,), (1,)), ((), ()))
TN = (((0,), (0,)), ((), ()))


def pass_kernel(
    cap,
    og_ref,
    rw_ref,
    rt_ref,
    sl_ref,
    ct_ref,
    sgate_ref,
    sup_ref,
    gw_ref,
    uw_ref,
    dw_ref,
    tok_ref,
    hid_out,
    rows_out,
    gw,
    uw,
    dw,
    sg,
    su,
    rows,
    far_out,
    up,
    fac_g,
    fac_u,
    hid,
    part,
    core_out,
    core_in,
    summed,
    quad_in,
    far_ret,
    far_in,
    near_ret,
    w_sem,
    l_sem,
    o_sem,
    sv_send,
    sv_recv,
    fd_send,
    fd_recv,
    qd_send,
    qd_recv,
    cd_send,
    cd_recv,
    cr_send,
    cr_recv,
    qr_send,
    qr_recv,
    fr_send,
    fr_recv,
):
    g = lax.axis_index("groups")
    e = lax.axis_index("expert")
    d = lax.axis_index("dp")
    half = e // QUAD
    r = e % QUAD
    far = (1 - half) * QUAD + r
    core_peer = (g, e, 1 - d)
    far_peer = (g, far, d)

    def quad_rank(rel):
        hi, lo = r // 2, r % 2
        if rel & 2:
            hi = 1 - hi
        if rel & 1:
            lo = 1 - lo
        return hi * 2 + lo

    def quad_peer(rel):
        return (g, half * QUAD + quad_rank(rel), d)

    ff = dw.shape[0]
    width = dw.shape[1]
    step = width // CHUNKS
    group = rows.shape[0] // 2

    mine = pl.multiple_of(d * ff, ff)
    loads = [
        pltpu.make_async_copy(sgate_ref.at[0, :, pl.ds(mine, ff)], sg.at[d], l_sem.at[0]),
        pltpu.make_async_copy(sup_ref.at[0, :, pl.ds(mine, ff)], su.at[d], l_sem.at[1]),
    ]
    for c in loads:
        c.start()
    w_dw = [
        pltpu.make_async_copy(
            dw_ref.at[pl.ds(mine, ff), pl.ds(c * step, step)],
            dw.at[:, pl.ds(c * step, step)],
            w_sem.at[0, c],
        )
        for c in range(CHUNKS)
    ]
    w_gw = [
        pltpu.make_async_copy(
            gw_ref.at[pl.ds(c * step, step), pl.ds(mine, ff)],
            gw.at[pl.ds(c * step, step), :],
            w_sem.at[1, c],
        )
        for c in range(CHUNKS)
    ]
    w_uw = [
        pltpu.make_async_copy(
            uw_ref.at[pl.ds(c * step, step), pl.ds(mine, ff)],
            uw.at[pl.ds(c * step, step), :],
            w_sem.at[2, c],
        )
        for c in range(CHUNKS)
    ]
    for c in range(CHUNKS):
        w_dw[c].start()
    for c in range(CHUNKS):
        w_gw[c].start()
        w_uw[c].start()

    barrier = pltpu.get_barrier_semaphore()
    for peer in (core_peer, far_peer, quad_peer(1), quad_peer(2), quad_peer(3)):
        pl.semaphore_signal(barrier, inc=1, device_id=peer, device_id_type=MESH)
    pl.semaphore_wait(barrier, 5)

    def remote(src, dst, ss, rs, peer):
        return pltpu.make_async_remote_copy(
            src_ref=src, dst_ref=dst, send_sem=ss, recv_sem=rs, device_id=peer, device_id_type=MESH
        )

    theirs = pl.multiple_of((1 - d) * ff, ff)
    saved = [
        remote(
            sgate_ref.at[0, :, pl.ds(theirs, ff)], sg.at[d], sv_send.at[0], sv_recv.at[0], core_peer
        ),
        remote(
            sup_ref.at[0, :, pl.ds(theirs, ff)], su.at[d], sv_send.at[1], sv_recv.at[1], core_peer
        ),
    ]

    tokens = og_ref.shape[0]
    lane = lax.broadcasted_iota(jnp.int32, (tokens, EXP_WIN * PAD), 1)
    lane_x = lane // PAD
    lane_c = lane % PAD
    live_count = jnp.where(lane_x == 0, ct_ref[0:1, 0:1], ct_ref[0:1, 1:2])
    match = [
        (rt_ref[:, k : k + 1] == lane_x) & (sl_ref[:, k : k + 1] == lane_c) & (lane_c < cap)
        for k in range(2)
    ]
    placing = [
        jnp.where(m & (lane_c < live_count), 1.0, 0.0).astype(BF16) for m in match
    ]

    def slot(owner):
        return pl.multiple_of(d * group + ((owner % QUAD) * 2 + owner // QUAD) * PAD, PAD)

    own_at = slot(e)
    far_at = slot(far)
    far_send, quad_near, quad_far, core_send = [], [], [], []
    for c in range(CHUNKS):
        cols = pl.ds(c * step, step)
        og = og_ref[:, cols].astype(F32)
        packed = jnp.zeros((EXP_WIN * PAD, step), F32)
        for k in range(2):
            scaled = (rw_ref[:, k : k + 1] * og).astype(BF16)
            packed = packed + lax.dot_general(placing[k], scaled, TN, preferred_element_type=F32)
        first, second = packed[:PAD], packed[PAD:]
        rows[pl.ds(own_at, PAD), cols] = jnp.where(half == 0, first, second).astype(BF16)
        far_out[:, cols] = jnp.where(half == 0, second, first).astype(BF16)
        cp = remote(
            far_out.at[:, cols],
            rows.at[pl.ds(own_at, PAD), cols],
            fd_send.at[c],
            fd_recv.at[c],
            far_peer,
        )
        cp.start()
        far_send.append(cp)
        near = []
        for rel in (1, 2, 3):
            cp = remote(
                rows.at[pl.ds(own_at, PAD), cols],
                rows.at[pl.ds(own_at, PAD), cols],
                qd_send.at[0, rel - 1, c],
                qd_recv.at[0, rel - 1, c],
                quad_peer(rel),
            )
            cp.start()
            near.append(cp)
        quad_near.append(near)
    for cp in saved:
        cp.start()

    for cp in loads:
        cp.wait()
    for cp in saved:
        cp.wait_recv()
    samples = sg.shape[1]
    ri = lax.broadcasted_iota(jnp.int32, (group, samples), 0)
    ci = lax.broadcasted_iota(jnp.int32, (group, samples), 1)
    block = ri // PAD
    place = ri % PAD
    owner = (block % 2) * QUAD + block // 2
    spread = jnp.where((ci == owner * cap + place) & (place < cap), 1.0, 0.0).astype(BF16)
    piece = 256
    for dd in range(2):
        for q in range(ff // piece):
            cols = pl.ds(q * piece, piece)
            at = pl.ds(dd * group, group)
            gv = jnp.dot(spread, sg[dd, :, cols], preferred_element_type=F32)
            uv = jnp.dot(spread, su[dd, :, cols], preferred_element_type=F32)
            s = jax.nn.sigmoid(gv)
            gs = gv * s
            fac_u[at, cols] = gs
            fac_g[at, cols] = uv * s * (1.0 + gv * (1.0 - s))
            hid[at, cols] = (gs * uv).astype(BF16)
    out_hid = pltpu.make_async_copy(hid, hid_out, o_sem.at[0])
    out_hid.start()

    for c in range(CHUNKS):
        cols = pl.ds(c * step, step)
        far_send[c].wait_recv()
        copies = []
        for rel in (1, 2, 3):
            cp = remote(
                rows.at[pl.ds(far_at, PAD), cols],
                rows.at[pl.ds(far_at, PAD), cols],
                qd_send.at[1, rel - 1, c],
                qd_recv.at[1, rel - 1, c],
                quad_peer(rel),
            )
            cp.start()
            copies.append(cp)
        quad_far.append(copies)

    own_rows = pl.ds(pl.multiple_of(d * group, group), group)
    other_rows = pl.ds(pl.multiple_of((1 - d) * group, group), group)

    def upstream_chunk(c):
        cols = pl.ds(c * step, step)
        core_send[c].wait_recv()
        w_dw[c].wait()
        term = lax.dot_general(rows[:, cols], dw[:, cols], NT, preferred_element_type=F32)
        if c == 0:
            up[...] = term
        else:
            up[...] += term

    for c in range(CHUNKS):
        cols = pl.ds(c * step, step)
        for rel in (1, 2, 3):
            quad_near[c][rel - 1].wait_recv()
            quad_far[c][rel - 1].wait_recv()
        cp = remote(
            rows.at[own_rows, cols],
            rows.at[own_rows, cols],
            cd_send.at[c],
            cd_recv.at[c],
            core_peer,
        )
        cp.start()
        core_send.append(cp)
        if c > 0:
            upstream_chunk(c - 1)
    upstream_chunk(CHUNKS - 1)
    out_rows = pltpu.make_async_copy(rows, rows_out, o_sem.at[1])
    out_rows.start()

    gg = (up[...] * fac_g[...]).astype(BF16)
    gu = (up[...] * fac_u[...]).astype(BF16)

    core_ret, quad_ret, far_back = [], [], []

    def stage_a(c):
        w_gw[c].wait()
        w_uw[c].wait()
        at = pl.ds(c * step, step)
        part[c] = lax.dot_general(gg, gw[at, :], NT, preferred_element_type=F32) + lax.dot_general(
            gu, uw[at, :], NT, preferred_element_type=F32
        )
        core_out[c] = part[c, other_rows, :].astype(BF16)
        cp = remote(core_out.at[c], core_in.at[c], cr_send.at[c], cr_recv.at[c], core_peer)
        cp.start()
        core_ret.append(cp)

    def stage_b(c):
        core_ret[c].wait_recv()
        summed[c] = (part[c, own_rows, :] + core_in[c].astype(F32)).astype(BF16)
        copies = []
        for rel in (1, 2, 3):
            at = pl.multiple_of(quad_rank(rel) * 2 * PAD, 2 * PAD)
            cp = remote(
                summed.at[c, pl.ds(at, 2 * PAD), :],
                quad_in.at[rel - 1, c],
                qr_send.at[rel - 1, c],
                qr_recv.at[rel - 1, c],
                quad_peer(rel),
            )
            cp.start()
            copies.append(cp)
        quad_ret.append(copies)

    def stage_c(c):
        for cp in quad_ret[c]:
            cp.wait_recv()
        at = pl.multiple_of(r * 2 * PAD, 2 * PAD)
        total = summed[c, pl.ds(at, 2 * PAD), :].astype(F32)
        for rel in (1, 2, 3):
            total = total + quad_in[rel - 1, c].astype(F32)
        first, second = total[:PAD], total[PAD:]
        near_ret[c] = jnp.where(half == 0, first, second)
        far_ret[c] = jnp.where(half == 0, second, first).astype(BF16)
        cp = remote(far_ret.at[c], far_in.at[c], fr_send.at[c], fr_recv.at[c], far_peer)
        cp.start()
        far_back.append(cp)

    table = jnp.where(match[0], 1.0, 0.0) + jnp.where(match[1], 1.0, 0.0)
    table_near = jnp.where(half == 0, table[:, :PAD], table[:, PAD:]).astype(BF16)
    table_far = jnp.where(half == 0, table[:, PAD:], table[:, :PAD]).astype(BF16)

    def stage_d(c):
        far_back[c].wait_recv()
        near = near_ret[c]
        high = near.astype(BF16)
        low = (near - high.astype(F32)).astype(BF16)
        total = jnp.dot(table_near, high, preferred_element_type=F32)
        total = total + jnp.dot(table_near, low, preferred_element_type=F32)
        total = total + jnp.dot(table_far, far_in[c], preferred_element_type=F32)
        tok_ref[:, pl.ds(c * step, step)] = total.astype(BF16)

    for c in range(CHUNKS + 3):
        if c < CHUNKS:
            stage_a(c)
        if 0 <= c - 1 < CHUNKS:
            stage_b(c - 1)
        if 0 <= c - 2 < CHUNKS:
            stage_c(c - 2)
        if 0 <= c - 3 < CHUNKS:
            stage_d(c - 3)

    out_hid.wait()
    out_rows.wait()
    for cp in saved + far_send + core_send + core_ret + far_back:
        cp.wait_send()
    for group_of in quad_near + quad_far + quad_ret:
        for cp in group_of:
            cp.wait_send()


def local_fast(og, rw, rt, sl, ct, sgate, sup, gw, uw, dw):
    tokens, width = og.shape
    ff = dw.shape[0] // 2
    samples = sgate.shape[1]
    owners = lax.axis_size("expert")
    cap = samples // owners
    group = owners * PAD
    step = width // CHUNKS
    vmem = pl.BlockSpec(memory_space=pltpu.VMEM)
    hbm = pl.BlockSpec(memory_space=pl.ANY)
    dma = pltpu.SemaphoreType.DMA
    tok, hid, rows = pl.pallas_call(
        functools.partial(pass_kernel, cap),
        out_shape=(
            jax.ShapeDtypeStruct((tokens, width), BF16),
            jax.ShapeDtypeStruct((2 * group, ff), BF16),
            jax.ShapeDtypeStruct((2 * group, width), BF16),
        ),
        in_specs=[vmem] * 5 + [hbm] * 5,
        out_specs=(vmem, hbm, hbm),
        scratch_shapes=[
            pltpu.VMEM((width, ff), BF16),
            pltpu.VMEM((width, ff), BF16),
            pltpu.VMEM((ff, width), BF16),
            pltpu.VMEM((2, samples, ff), BF16),
            pltpu.VMEM((2, samples, ff), BF16),
            pltpu.VMEM((2 * group, width), BF16),
            pltpu.VMEM((PAD, width), BF16),
            pltpu.VMEM((2 * group, ff), F32),
            pltpu.VMEM((2 * group, ff), F32),
            pltpu.VMEM((2 * group, ff), F32),
            pltpu.VMEM((2 * group, ff), BF16),
            pltpu.VMEM((CHUNKS, 2 * group, step), F32),
            pltpu.VMEM((CHUNKS, group, step), BF16),
            pltpu.VMEM((CHUNKS, group, step), BF16),
            pltpu.VMEM((CHUNKS, group, step), BF16),
            pltpu.VMEM((3, CHUNKS, 2 * PAD, step), BF16),
            pltpu.VMEM((CHUNKS, PAD, step), BF16),
            pltpu.VMEM((CHUNKS, PAD, step), BF16),
            pltpu.VMEM((CHUNKS, PAD, step), F32),
            dma((3, CHUNKS)),
            dma((2,)),
            dma((2,)),
            dma((2,)),
            dma((2,)),
            dma((CHUNKS,)),
            dma((CHUNKS,)),
            dma((2, 3, CHUNKS)),
            dma((2, 3, CHUNKS)),
            dma((CHUNKS,)),
            dma((CHUNKS,)),
            dma((CHUNKS,)),
            dma((CHUNKS,)),
            dma((3, CHUNKS)),
            dma((3, CHUNKS)),
            dma((CHUNKS,)),
            dma((CHUNKS,)),
        ],
        compiler_params=pltpu.CompilerParams(
            collective_id=0, has_side_effects=True, vmem_limit_bytes=52 * 1024 * 1024
        ),
        cost_estimate=pl.CostEstimate(
            flops=12 * group * ff * width, bytes_accessed=6 * ff * width, transcendentals=2 * group * ff
        ),
    )(og, rw, rt, sl, ct, sgate, sup, gw, uw, dw)
    down = lax.dot_general(hid, rows, TN, preferred_element_type=F32)
    return tok, down


def local_plain(og, rw, rt, sl, ct, sgate, sup, gw, uw, dw):
    senders = lax.axis_size("expert")
    shards = senders // EXP_WIN
    capacity = sgate.shape[1] // senders
    tokens, width = og.shape
    places = jnp.arange(capacity, dtype=jnp.int32)
    experts = jnp.arange(EXP_WIN, dtype=jnp.int32)
    matches = (rt[:, :, None, None] == experts[None, None, :, None]) & (
        sl[:, :, None, None] == places[None, None, None, :]
    )
    live = places[None, :] < ct[0][:, None]
    scaled = (rw[:, :, None] * og[:, None, :].astype(F32)).astype(BF16)
    placing = (matches & live[None, None, :, :]).astype(BF16)
    packed = jnp.einsum("tkxc,tkd->xcd", placing, scaled, preferred_element_type=F32).astype(BF16)
    outgoing = jnp.repeat(packed, shards, axis=0)
    arrived = lax.all_to_all(outgoing, "expert", split_axis=0, concat_axis=0, tiled=True)
    rows = arrived.reshape(senders * capacity, width)
    gv = sgate[0].astype(F32)
    uv = sup[0].astype(F32)
    upstream = lax.dot_general(rows, dw, NT, preferred_element_type=F32)
    s = jax.nn.sigmoid(gv)
    grad_up = (upstream * gv * s).astype(BF16)
    grad_gate = (upstream * uv * s * (1.0 + gv * (1.0 - s))).astype(BF16)
    hidden = (gv * s * uv).astype(BF16)
    part = lax.dot_general(grad_gate, gw, NT, preferred_element_type=F32)
    part = part + lax.dot_general(grad_up, uw, NT, preferred_element_type=F32)
    table = jnp.sum(matches.astype(F32), axis=1).reshape(tokens, EXP_WIN * capacity)
    received = lax.all_to_all(
        part.astype(BF16).reshape(senders, capacity, width),
        "expert",
        split_axis=0,
        concat_axis=0,
        tiled=True,
    )
    summed = jnp.sum(received.reshape(EXP_WIN, shards, capacity, width), axis=1, dtype=F32)
    gathered = jnp.dot(
        table,
        summed.reshape(EXP_WIN * capacity, width),
        precision=lax.Precision.HIGHEST,
        preferred_element_type=F32,
    )
    both_hidden = lax.all_to_all(hidden, "dp", split_axis=1, concat_axis=0, tiled=True)
    both_rows = lax.all_gather(rows, "dp", axis=0, tiled=True)
    down = lax.dot_general(both_hidden, both_rows, TN, preferred_element_type=F32)
    return gathered.astype(BF16), down


def solution(mesh):
    tokens = P(("groups", "expert", "dp"), None)
    saved = P(("groups", "dp"), None, "expert")
    columns = P(None, "expert")
    fits = mesh.shape["expert"] == EXP_WIN * QUAD and mesh.shape["dp"] == 2
    return jax.shard_map(
        local_fast if fits else local_plain,
        mesh=mesh,
        in_specs=(tokens,) * 5 + (saved, saved, columns, columns, P("expert", None)),
        out_specs=(tokens, tokens),
        check_vma=False,
    )
```

time: 133 us -> 64.6 us (0.49)
  Pallas kernels: 0 us -> 47.7 us
  matrix products: 51.2 us -> 10.2 us
  blocking collectives: 32.8 us -> 0 us
  waiting for transfers between devices: 24.8 us -> 0 us
  between operations: 14.1 us -> 0.64 us
  starting transfers between devices: 3.68 us -> 0 us
  other arithmetic: 3.41 us -> 0 us
  local copies, waits for them, and re-layouts: 2.53 us -> 5.74 us
    pallas_call x0 -> x1, Pallas kernels: none -> 47.7 us  [local_fast(): pl.pallas_call(functools.partial(pass_kernel, cap), out_shape=(jax.ShapeD...]
    dot_general x5 -> x1, matrix products: 51.2 us -> 10.2 us  [local_fast(): down = lax.dot_general(hid, rows, TN, preferred_element_type=F32)]
    all_to_all x1 -> x0, blocking collectives: 32.8 us -> none  [local(): lax.all_to_all(outgoing, 'expert', split_axis=0, concat_axis=0, tiled=True)]
    all_to_all x1 -> x0, waiting for transfers between devices: 24.8 us -> none  [local(): lax.all_to_all(partial_value.reshape(senders, capacity, width), 'expert',...]
    unnamed x4 -> x10, local copies, waits for them, and re-layouts: 1.09 us -> 5.74 us
    all_to_all x1 -> x0, starting transfers between devices: 3.65 us -> none  [local(): lax.all_to_all(partial_value.reshape(senders, capacity, width), 'expert',...]
    eq x2 -> x0, other arithmetic: 1.37 us -> none  [the longest x1 0.69 us: local(): route_slots[:, :, None, None] == places[None, None, None, :]]
    reshape x2 -> x0, local copies, waits for them, and re-layouts: 1.34 us -> none  [the longest x1 1.16 us: local(): partial_value.reshape(senders, capacity, width)]
  transfers between devices with their start and end apart: 2 -> 0, of which waited for: 1 -> 0; matrix products, arithmetic and copies ran while one was open for 28% -> 0% of each run, Pallas kernels for 0% -> 0%
where the time goes in v1:
time: 64.6 us; the launch traced here: 64.3 us
  Pallas kernels  47.7 us (74%)
  matrix products  10.2 us (16%)
  local copies, waits for them, and re-layouts  5.74 us (9%)
    pallas_call x1, Pallas kernels, local_fast(): pl.pallas_call(functools.partial(pass_kernel, cap), out_shape=(jax.ShapeD...  47.7 us
    dot_general x1, matrix products, local_fast(): down = lax.dot_general(hid, rows, TN, preferred_element_type=F32)  10.2 us
    unnamed x10, local copies, waits for them, and re-layouts  5.74 us

profile of v1, /device:TPU:0, one launch (start us, length us, event | category | flops | bytes accessed | tf_op | source)
XLA Modules:
  0.0 64.3 jit_solution(16272300587800985273)
XLA Ops:
  0.6 0.8 %copy.12.rw_ref = f32[64,2]{1,0:T(8,128)S(1)} copy(f32[64,2]{0,1:T(2,128)} %param.11) | data formatting | bytes 1024 | tf_op args[1]
  1.4 0.8 %copy.13.rt_ref = s32[64,2]{1,0:T(8,128)S(1)} copy(s32[64,2]{0,1:T(2,128)} %param.12) | data formatting | bytes 1024 | tf_op args[2]
  2.2 0.8 %copy.14.sl_ref = s32[64,2]{1,0:T(8,128)S(1)} copy(s32[64,2]{0,1:T(2,128)} %param.13) | data formatting | bytes 1024 | tf_op args[3]
  2.9 0.0 copy-start
  2.9 1.0 %copy-done = bf16[1,96,2048]{2,1,0:T(8,128)(2,1)S(1)} copy-done((bf16[1,96,2048]{2,1,0:T(8,128)(2,1)S(1)}, bf16[1,96,2048]{2,1,0:T(8,128)(2,1)}, u32[]{:S(2)}) %copy-start) | copy-done | bytes 393240
  3.9 0.0 copy-start.1
  3.9 1.0 %copy-done.1 = bf16[1,96,2048]{2,1,0:T(8,128)(2,1)S(1)} copy-done((bf16[1,96,2048]{2,1,0:T(8,128)(2,1)S(1)}, bf16[1,96,2048]{2,1,0:T(8,128)(2,1)}, u32[]{:S(2)}) %copy-start.1) | copy-done | bytes 393240
  4.9 0.0 copy-start.2
  4.9 0.7 %copy-done.2 = s32[1,2]{1,0:T(1,128)S(1)} copy-done((s32[1,2]{1,0:T(1,128)S(1)}, s32[1,2]{1,0:T(1,128)}, u32[]{:S(2)}) %copy-start.2) | copy-done | bytes 32
  5.6 47.7 %shard_map.113 = (bf16[64,4096]{1,0:T(8,128)(2,1)S(1)}, bf16[256,1024]{1,0:T(8,128)(2,1)S(1)}, bf16[256,4096]{1,0:T(8,128)(2,1)}) custom-call(bf16[64,4096]{1,0:T(8,128)(2,1)} %og_ref.1, f32[64,2]{1,0:T(8,128)S(1)} %copy.12.rw_ref, s32[64,2]{1,0:T(8,128)S(1)} %copy.13.rt_ref, s32[64,2]{1,0:T(8,128)S(1)} %copy.14.sl_ref, s32[1,2]{1,0:T(1,128)S(1)} %copy-done.2, ...), custom_call_target="tpu_custom_call" | custom-call | flops 6442450944 | bytes 25165824 | tf_op jit(solution)/shard_map/pallas_call | solution.py:375
  53.3 10.2 %fusion = f32[1024,4096]{1,0:T(8,128)} fusion(bf16[256,1024]{1,0:T(8,128)(2,1)S(1)} %get-tuple-element.6, bf16[256,4096]{1,0:T(8,128)(2,1)} %get-tuple-element.7), kind=kOutput, calls=%fused_computation | convolution fusion | flops 2147483648 | bytes 19398656 | tf_op jit(solution)/shard_map/dot_general | solution.py:429
  63.5 0.8 %copy.16 = bf16[64,4096]{1,0:T(8,128)(2,1)} copy(bf16[64,4096]{1,0:T(8,128)(2,1)S(1)} %get-tuple-element.10) | data formatting | bytes 1048576
Async XLA Ops:
  2.9 1.0 %copy-start = (bf16[1,96,2048]{2,1,0:T(8,128)(2,1)S(1)}, bf16[1,96,2048]{2,1,0:T(8,128)(2,1)}, u32[]{:S(2)}) copy-start(bf16[1,96,2048]{2,1,0:T(8,128)(2,1)} %sgate_ref.1) | copy-start | bytes 1179652
  3.9 1.0 %copy-start.1 = (bf16[1,96,2048]{2,1,0:T(8,128)(2,1)S(1)}, bf16[1,96,2048]{2,1,0:T(8,128)(2,1)}, u32[]{:S(2)}) copy-start(bf16[1,96,2048]{2,1,0:T(8,128)(2,1)} %sup_ref.1) | copy-start | bytes 1179652
  4.9 0.7 %copy-start.2 = (s32[1,2]{1,0:T(1,128)S(1)}, s32[1,2]{1,0:T(1,128)}, u32[]{:S(2)}) copy-start(s32[1,2]{1,0:T(1,128)} %ct_ref.1) | copy-start | bytes 28

commit v2 on v1

--- a/solution.py
+++ b/solution.py
@@ -10,7 +10,10 @@
 EXP_WIN = 2
 QUAD = 4
 PAD = 16
-CHUNKS = 4
+CHUNKS = 2
+DOWN_STEPS = 4
+RELAY = (2, 1)
+RELAY_BACK = (1, 2)
 MESH = pl.DeviceIdType.MESH
 F32 = jnp.float32
 BF16 = jnp.bfloat16
@@ -20,11 +23,11 @@
 
 def pass_kernel(
     cap,
-    og_ref,
-    rw_ref,
-    rt_ref,
-    sl_ref,
-    ct_ref,
+    og_hbm,
+    rw_hbm,
+    rt_hbm,
+    sl_hbm,
+    ct_hbm,
     sgate_ref,
     sup_ref,
     gw_ref,
@@ -33,6 +36,12 @@
     tok_ref,
     hid_out,
     rows_out,
+    og_ref,
+    rw_ref,
+    rt_ref,
+    sl_ref,
+    ct_ref,
+    in_sem,
     gw,
     uw,
     dw,
@@ -49,6 +58,7 @@
     core_in,
     summed,
     quad_in,
+    relayed,
     far_ret,
     far_in,
     near_ret,
@@ -95,6 +105,20 @@
     step = width // CHUNKS
     group = rows.shape[0] // 2
 
+    small = [
+        pltpu.make_async_copy(src, dst, in_sem.at[i])
+        for i, (src, dst) in enumerate(
+            (
+                (rt_hbm, rt_ref),
+                (sl_hbm, sl_ref),
+                (ct_hbm, ct_ref),
+                (rw_hbm, rw_ref),
+                (og_hbm, og_ref),
+            )
+        )
+    ]
+    for c in small:
+        c.start()
     mine = pl.multiple_of(d * ff, ff)
     loads = [
         pltpu.make_async_copy(sgate_ref.at[0, :, pl.ds(mine, ff)], sg.at[d], l_sem.at[0]),
@@ -126,16 +150,10 @@
         )
         for c in range(CHUNKS)
     ]
-    for c in range(CHUNKS):
-        w_dw[c].start()
-    for c in range(CHUNKS):
-        w_gw[c].start()
-        w_uw[c].start()
-
     barrier = pltpu.get_barrier_semaphore()
-    for peer in (core_peer, far_peer, quad_peer(1), quad_peer(2), quad_peer(3)):
+    for peer in (core_peer, far_peer, quad_peer(1), quad_peer(2)):
         pl.semaphore_signal(barrier, inc=1, device_id=peer, device_id_type=MESH)
-    pl.semaphore_wait(barrier, 5)
+    pl.semaphore_wait(barrier, 4)
 
     def remote(src, dst, ss, rs, peer):
         return pltpu.make_async_remote_copy(
@@ -152,32 +170,50 @@
         ),
     ]
 
+    for c in small:
+        c.wait()
     tokens = og_ref.shape[0]
-    lane = lax.broadcasted_iota(jnp.int32, (tokens, EXP_WIN * PAD), 1)
-    lane_x = lane // PAD
-    lane_c = lane % PAD
-    live_count = jnp.where(lane_x == 0, ct_ref[0:1, 0:1], ct_ref[0:1, 1:2])
+    line = lax.broadcasted_iota(jnp.int32, (EXP_WIN * PAD, tokens), 0)
+    line_x = line // PAD
+    line_c = line % PAD
+    live_count = jnp.where(line_x == 0, ct_ref[0:1, 0:1], ct_ref[0:1, 1:2])
     match = [
-        (rt_ref[:, k : k + 1] == lane_x) & (sl_ref[:, k : k + 1] == lane_c) & (lane_c < cap)
+        (rt_ref[k : k + 1, :] == line_x) & (sl_ref[k : k + 1, :] == line_c) & (line_c < cap)
         for k in range(2)
     ]
     placing = [
-        jnp.where(m & (lane_c < live_count), 1.0, 0.0).astype(BF16) for m in match
+        jnp.where(m & (line_c < live_count), 1.0, 0.0).astype(BF16) for m in match
+    ]
+    same = lax.broadcasted_iota(jnp.int32, (tokens, tokens), 0) == lax.broadcasted_iota(
+        jnp.int32, (tokens, tokens), 1
+    )
+    weight = [
+        jnp.sum(jnp.where(same, rw_ref[k : k + 1, :], 0.0), axis=1, keepdims=True)
+        for k in range(2)
     ]
 
     def slot(owner):
         return pl.multiple_of(d * group + ((owner % QUAD) * 2 + owner // QUAD) * PAD, PAD)
+
+    def quad_copy(at, kind, source, c, rel):
+        place = rows.at[pl.ds(at, PAD), pl.ds(c * step, step)]
+        cp = remote(
+            place, place, qd_send.at[kind, source, c], qd_recv.at[kind, source, c], quad_peer(rel)
+        )
+        cp.start()
+        return cp
 
     own_at = slot(e)
     far_at = slot(far)
     far_send, quad_near, quad_far, core_send = [], [], [], []
+    relay_near, relay_far = [], []
     for c in range(CHUNKS):
         cols = pl.ds(c * step, step)
         og = og_ref[:, cols].astype(F32)
         packed = jnp.zeros((EXP_WIN * PAD, step), F32)
         for k in range(2):
-            scaled = (rw_ref[:, k : k + 1] * og).astype(BF16)
-            packed = packed + lax.dot_general(placing[k], scaled, TN, preferred_element_type=F32)
+            scaled = (weight[k] * og).astype(BF16)
+            packed = packed + jnp.dot(placing[k], scaled, preferred_element_type=F32)
         first, second = packed[:PAD], packed[PAD:]
         rows[pl.ds(own_at, PAD), cols] = jnp.where(half == 0, first, second).astype(BF16)
         far_out[:, cols] = jnp.where(half == 0, second, first).astype(BF16)
@@ -190,20 +226,11 @@
         )
         cp.start()
         far_send.append(cp)
-        near = []
-        for rel in (1, 2, 3):
-            cp = remote(
-                rows.at[pl.ds(own_at, PAD), cols],
-                rows.at[pl.ds(own_at, PAD), cols],
-                qd_send.at[0, rel - 1, c],
-                qd_recv.at[0, rel - 1, c],
-                quad_peer(rel),
-            )
-            cp.start()
-            near.append(cp)
-        quad_near.append(near)
+        quad_near.append([quad_copy(own_at, 0, rel - 1, c, rel) for rel in (1, 2)])
     for cp in saved:
         cp.start()
+    for c in range(CHUNKS):
+        w_dw[c].start()
 
     for cp in loads:
         cp.wait()
@@ -217,6 +244,13 @@
     owner = (block % 2) * QUAD + block // 2
     spread = jnp.where((ci == owner * cap + place) & (place < cap), 1.0, 0.0).astype(BF16)
     piece = 256
+
+    def relay(c, sent, kind):
+        via = RELAY[c]
+        sent[c][via - 1].wait_recv()
+        source = (half if kind == 0 else 1 - half) * QUAD + quad_rank(via)
+        return quad_copy(slot(source), kind, 2, c, 3 - via)
+
     for dd in range(2):
         for q in range(ff // piece):
             cols = pl.ds(q * piece, piece)
@@ -227,25 +261,11 @@
             gs = gv * s
             fac_u[at, cols] = gs
             fac_g[at, cols] = uv * s * (1.0 + gv * (1.0 - s))
-            hid[at, cols] = (gs * uv).astype(BF16)
+            hid[cols, at] = jnp.transpose(gs * uv).astype(BF16)
+            if dd == 1 and q < CHUNKS:
+                relay_near.append(relay(q, quad_near, 0))
     out_hid = pltpu.make_async_copy(hid, hid_out, o_sem.at[0])
     out_hid.start()
-
-    for c in range(CHUNKS):
-        cols = pl.ds(c * step, step)
-        far_send[c].wait_recv()
-        copies = []
-        for rel in (1, 2, 3):
-            cp = remote(
-                rows.at[pl.ds(far_at, PAD), cols],
-                rows.at[pl.ds(far_at, PAD), cols],
-                qd_send.at[1, rel - 1, c],
-                qd_recv.at[1, rel - 1, c],
-                quad_peer(rel),
-            )
-            cp.start()
-            copies.append(cp)
-        quad_far.append(copies)
 
     own_rows = pl.ds(pl.multiple_of(d * group, group), group)
     other_rows = pl.ds(pl.multiple_of((1 - d) * group, group), group)
@@ -260,23 +280,33 @@
         else:
             up[...] += term
 
-    for c in range(CHUNKS):
-        cols = pl.ds(c * step, step)
-        for rel in (1, 2, 3):
-            quad_near[c][rel - 1].wait_recv()
-            quad_far[c][rel - 1].wait_recv()
-        cp = remote(
-            rows.at[own_rows, cols],
-            rows.at[own_rows, cols],
-            cd_send.at[c],
-            cd_recv.at[c],
-            core_peer,
-        )
-        cp.start()
-        core_send.append(cp)
-        if c > 0:
-            upstream_chunk(c - 1)
-    upstream_chunk(CHUNKS - 1)
+    for t in range(CHUNKS + 3):
+        if t < CHUNKS:
+            far_send[t].wait_recv()
+            quad_far.append([quad_copy(far_at, 1, rel - 1, t, rel) for rel in (1, 2)])
+            w_gw[t].start()
+            w_uw[t].start()
+        if 0 <= t - 1 < CHUNKS:
+            relay_far.append(relay(t - 1, quad_far, 1))
+        if 0 <= t - 2 < CHUNKS:
+            c = t - 2
+            cols = pl.ds(c * step, step)
+            straight = 2 - RELAY[c]
+            quad_near[c][straight].wait_recv()
+            quad_far[c][straight].wait_recv()
+            relay_near[c].wait_recv()
+            relay_far[c].wait_recv()
+            cp = remote(
+                rows.at[own_rows, cols],
+                rows.at[own_rows, cols],
+                cd_send.at[c],
+                cd_recv.at[c],
+                core_peer,
+            )
+            cp.start()
+            core_send.append(cp)
+        if t >= 3:
+            upstream_chunk(t - 3)
     out_rows = pltpu.make_async_copy(rows, rows_out, o_sem.at[1])
     out_rows.start()
 
@@ -300,27 +330,39 @@
     def stage_b(c):
         core_ret[c].wait_recv()
         summed[c] = (part[c, own_rows, :] + core_in[c].astype(F32)).astype(BF16)
+        via = RELAY_BACK[c]
         copies = []
-        for rel in (1, 2, 3):
-            at = pl.multiple_of(quad_rank(rel) * 2 * PAD, 2 * PAD)
+        for i, rank in enumerate((quad_rank(via), quad_rank(3))):
             cp = remote(
-                summed.at[c, pl.ds(at, 2 * PAD), :],
-                quad_in.at[rel - 1, c],
-                qr_send.at[rel - 1, c],
-                qr_recv.at[rel - 1, c],
-                quad_peer(rel),
+                summed.at[c, pl.ds(pl.multiple_of(rank * 2 * PAD, 2 * PAD), 2 * PAD), :],
+                quad_in.at[i, c],
+                qr_send.at[i, c],
+                qr_recv.at[i, c],
+                quad_peer(via),
             )
             cp.start()
             copies.append(cp)
         quad_ret.append(copies)
 
+    def stage_r(c):
+        rel = 3 - RELAY_BACK[c]
+        quad_ret[c][1].wait_recv()
+        at = pl.multiple_of(quad_rank(rel) * 2 * PAD, 2 * PAD)
+        relayed[c] = (
+            summed[c, pl.ds(at, 2 * PAD), :].astype(F32) + quad_in[1, c].astype(F32)
+        ).astype(BF16)
+        cp = remote(
+            relayed.at[c], quad_in.at[2, c], qr_send.at[2, c], qr_recv.at[2, c], quad_peer(rel)
+        )
+        cp.start()
+        quad_ret[c].append(cp)
+
     def stage_c(c):
-        for cp in quad_ret[c]:
-            cp.wait_recv()
+        quad_ret[c][0].wait_recv()
+        quad_ret[c][2].wait_recv()
         at = pl.multiple_of(r * 2 * PAD, 2 * PAD)
         total = summed[c, pl.ds(at, 2 * PAD), :].astype(F32)
-        for rel in (1, 2, 3):
-            total = total + quad_in[rel - 1, c].astype(F32)
+        total = total + quad_in[0, c].astype(F32) + quad_in[2, c].astype(F32)
         first, second = total[:PAD], total[PAD:]
         near_ret[c] = jnp.where(half == 0, first, second)
         far_ret[c] = jnp.where(half == 0, second, first).astype(BF16)
@@ -329,36 +371,35 @@
         far_back.append(cp)
 
     table = jnp.where(match[0], 1.0, 0.0) + jnp.where(match[1], 1.0, 0.0)
-    table_near = jnp.where(half == 0, table[:, :PAD], table[:, PAD:]).astype(BF16)
-    table_far = jnp.where(half == 0, table[:, PAD:], table[:, :PAD]).astype(BF16)
+    table_near = jnp.where(half == 0, table[:PAD], table[PAD:]).astype(BF16)
+    table_far = jnp.where(half == 0, table[PAD:], table[:PAD]).astype(BF16)
 
     def stage_d(c):
         far_back[c].wait_recv()
         near = near_ret[c]
         high = near.astype(BF16)
         low = (near - high.astype(F32)).astype(BF16)
-        total = jnp.dot(table_near, high, preferred_element_type=F32)
-        total = total + jnp.dot(table_near, low, preferred_element_type=F32)
-        total = total + jnp.dot(table_far, far_in[c], preferred_element_type=F32)
+        total = lax.dot_general(table_near, high, TN, preferred_element_type=F32)
+        total = total + lax.dot_general(table_near, low, TN, preferred_element_type=F32)
+        total = total + lax.dot_general(table_far, far_in[c], TN, preferred_element_type=F32)
         tok_ref[:, pl.ds(c * step, step)] = total.astype(BF16)
 
-    for c in range(CHUNKS + 3):
-        if c < CHUNKS:
-            stage_a(c)
-        if 0 <= c - 1 < CHUNKS:
-            stage_b(c - 1)
-        if 0 <= c - 2 < CHUNKS:
-            stage_c(c - 2)
-        if 0 <= c - 3 < CHUNKS:
-            stage_d(c - 3)
+    for t in range(CHUNKS + 4):
+        for lag, stage in enumerate((stage_a, stage_b, stage_r, stage_c, stage_d)):
+            if 0 <= t - lag < CHUNKS:
+                stage(t - lag)
 
     out_hid.wait()
     out_rows.wait()
-    for cp in saved + far_send + core_send + core_ret + far_back:
+    for cp in saved + far_send + relay_near + relay_far + core_send + core_ret + far_back:
         cp.wait_send()
     for group_of in quad_near + quad_far + quad_ret:
         for cp in group_of:
             cp.wait_send()
+
+
+def down_kernel(hid_ref, rows_ref, out_ref):
+    out_ref[...] = jnp.dot(hid_ref[...], rows_ref[...], preferred_element_type=F32)
 
 
 def local_fast(og, rw, rt, sl, ct, sgate, sup, gw, uw, dw):
@@ -376,12 +417,18 @@
         functools.partial(pass_kernel, cap),
         out_shape=(
             jax.ShapeDtypeStruct((tokens, width), BF16),
-            jax.ShapeDtypeStruct((2 * group, ff), BF16),
+            jax.ShapeDtypeStruct((ff, 2 * group), BF16),
             jax.ShapeDtypeStruct((2 * group, width), BF16),
         ),
-        in_specs=[vmem] * 5 + [hbm] * 5,
+        in_specs=[hbm] * 10,
         out_specs=(vmem, hbm, hbm),
         scratch_shapes=[
+            pltpu.VMEM(og.shape, BF16),
+            pltpu.VMEM((2, tokens), F32),
+            pltpu.VMEM((2, tokens), jnp.int32),
+            pltpu.VMEM((2, tokens), jnp.int32),
+            pltpu.VMEM(ct.shape, jnp.int32),
+            dma((5,)),
             pltpu.VMEM((width, ff), BF16),
             pltpu.VMEM((width, ff), BF16),
             pltpu.VMEM((ff, width), BF16),
@@ -392,12 +439,13 @@
             pltpu.VMEM((2 * group, ff), F32),
             pltpu.VMEM((2 * group, ff), F32),
             pltpu.VMEM((2 * group, ff), F32),
-            pltpu.VMEM((2 * group, ff), BF16),
+            pltpu.VMEM((ff, 2 * group), BF16),
             pltpu.VMEM((CHUNKS, 2 * group, step), F32),
             pltpu.VMEM((CHUNKS, group, step), BF16),
             pltpu.VMEM((CHUNKS, group, step), BF16),
             pltpu.VMEM((CHUNKS, group, step), BF16),
             pltpu.VMEM((3, CHUNKS, 2 * PAD, step), BF16),
+            pltpu.VMEM((CHUNKS, 2 * PAD, step), BF16),
             pltpu.VMEM((CHUNKS, PAD, step), BF16),
             pltpu.VMEM((CHUNKS, PAD, step), BF16),
             pltpu.VMEM((CHUNKS, PAD, step), F32),
@@ -420,13 +468,27 @@
             dma((CHUNKS,)),
         ],
         compiler_params=pltpu.CompilerParams(
-            collective_id=0, has_side_effects=True, vmem_limit_bytes=52 * 1024 * 1024
+            collective_id=0, has_side_effects=True, vmem_limit_bytes=60 * 1024 * 1024
         ),
         cost_estimate=pl.CostEstimate(
             flops=12 * group * ff * width, bytes_accessed=6 * ff * width, transcendentals=2 * group * ff
         ),
-    )(og, rw, rt, sl, ct, sgate, sup, gw, uw, dw)
-    down = lax.dot_general(hid, rows, TN, preferred_element_type=F32)
+    )(og, rw.T, rt.T, sl.T, ct, sgate, sup, gw, uw, dw)
+    tile = width // DOWN_STEPS
+    down = pl.pallas_call(
+        down_kernel,
+        grid=(DOWN_STEPS,),
+        in_specs=[
+            pl.BlockSpec((ff, 2 * group), lambda i: (0, 0)),
+            pl.BlockSpec((2 * group, tile), lambda i: (0, i)),
+        ],
+        out_specs=pl.BlockSpec((ff, tile), lambda i: (0, i)),
+        out_shape=jax.ShapeDtypeStruct((ff, width), F32),
+        compiler_params=pltpu.CompilerParams(vmem_limit_bytes=62 * 1024 * 1024),
+        cost_estimate=pl.CostEstimate(
+            flops=4 * group * ff * width, bytes_accessed=4 * ff * width, transcendentals=0
+        ),
+    )(hid, rows)
     return tok, down
 
 

time: 64.6 us -> 59.4 us (0.920)
  matrix products: 10.2 us -> 0 us
  Pallas kernels: 47.7 us -> 57.7 us
  local copies, waits for them, and re-layouts: 5.74 us -> 0.8 us
    dot_general x1 -> x0, matrix products: 10.2 us -> none  [local_fast(): down = lax.dot_general(hid, rows, TN, preferred_element_type=F32)]
    pallas_call x0 -> x1, Pallas kernels: none -> 8.12 us  [local_fast(): pl.pallas_call(down_kernel, grid=(DOWN_STEPS,), in_specs=[pl.BlockSpec((f...]
    unnamed x10 -> x3, local copies, waits for them, and re-layouts: 5.74 us -> 0.8 us
    pallas_call x1, Pallas kernels: 47.7 us -> 49.6 us  [local_fast(): pl.pallas_call(functools.partial(pass_kernel, cap), out_shape=(jax.ShapeD...]
where the time goes in v2:
time: 59.4 us; the launch traced here: 59.2 us
  Pallas kernels  57.7 us (97%)
  local copies, waits for them, and re-layouts  0.8 us (1%)
  between operations  0.65 us (1%)
    pallas_call x1, Pallas kernels, local_fast(): pl.pallas_call(functools.partial(pass_kernel, cap), out_shape=(jax.ShapeD...  49.6 us
    pallas_call x1, Pallas kernels, local_fast(): pl.pallas_call(down_kernel, grid=(DOWN_STEPS,), in_specs=[pl.BlockSpec((f...  8.12 us

profile of v2, /device:TPU:0, one launch (start us, length us, event | category | flops | bytes accessed | tf_op | source)
XLA Modules:
  0.0 59.2 jit_solution(1302222838269174381)
XLA Ops:
  0.6 49.6 %shard_map.113 = (bf16[64,4096]{1,0:T(8,128)(2,1)}, bf16[1024,256]{1,0:T(8,128)(2,1)}, bf16[256,4096]{1,0:T(8,128)(2,1)}) custom-call(bf16[64,4096]{1,0:T(8,128)(2,1)} %og_hbm.1, f32[2,64]{1,0:T(2,128)} %bitcast.3, s32[2,64]{1,0:T(2,128)} %bitcast.4, s32[2,64]{1,0:T(2,128)} %bitcast.5, s32[1,2]{1,0:T(1,128)} %ct_hbm.1, bf16[1,96,2048]{2,1,0:T(8,128)(2,1)} %sgate_ref.1, ...), custom_call_target="tpu_custom_call" | custom-call | flops 6442450944 | bytes 25165824 | tf_op jit(solution)/shard_map/pallas_call | solution.py:416
  50.2 0.0 copy-start
  50.3 8.1 %shard_map.114 = f32[1024,4096]{1,0:T(8,128)} custom-call(bf16[1024,256]{1,0:T(8,128)(2,1)} %get-tuple-element.6.hid_ref, bf16[256,4096]{1,0:T(8,128)(2,1)} %get-tuple-element.7.rows_ref), custom_call_target="tpu_custom_call" | custom-call | flops 2147483648 | bytes 16777216 | tf_op jit(solution)/shard_map/pallas_call | solution.py:478
  58.4 0.0 copy-done
  58.4 0.8 %copy.13 = bf16[64,4096]{1,0:T(8,128)(2,1)} copy(bf16[64,4096]{1,0:T(8,128)(2,1)S(1)} %copy-done) | data formatting | bytes 1048576
Async XLA Ops:
  50.2 8.1 %copy-start = (bf16[64,4096]{1,0:T(8,128)(2,1)S(1)}, bf16[64,4096]{1,0:T(8,128)(2,1)}, u32[]{:S(2)}) copy-start(bf16[64,4096]{1,0:T(8,128)(2,1)} %get-tuple-element.10) | copy-start | bytes 1572868

commit v3 on v2

--- a/solution.py
+++ b/solution.py
@@ -315,13 +315,21 @@
 
     core_ret, quad_ret, far_back = [], [], []
 
-    def stage_a(c):
+    sub = step // 2
+
+    def stage_first(c):
         w_gw[c].wait()
         w_uw[c].wait()
-        at = pl.ds(c * step, step)
-        part[c] = lax.dot_general(gg, gw[at, :], NT, preferred_element_type=F32) + lax.dot_general(
-            gu, uw[at, :], NT, preferred_element_type=F32
-        )
+        returned_piece(c, 0)
+
+    def returned_piece(c, piece):
+        at = pl.ds(c * step + piece * sub, sub)
+        part[c, :, pl.ds(piece * sub, sub)] = lax.dot_general(
+            gg, gw[at, :], NT, preferred_element_type=F32
+        ) + lax.dot_general(gu, uw[at, :], NT, preferred_element_type=F32)
+
+    def stage_a(c):
+        returned_piece(c, 1)
         core_out[c] = part[c, other_rows, :].astype(BF16)
         cp = remote(core_out.at[c], core_in.at[c], cr_send.at[c], cr_recv.at[c], core_peer)
         cp.start()
@@ -385,7 +393,8 @@
         tok_ref[:, pl.ds(c * step, step)] = total.astype(BF16)
 
     for t in range(CHUNKS + 4):
-        for lag, stage in enumerate((stage_a, stage_b, stage_r, stage_c, stage_d)):
+        order = (stage_first, stage_b, stage_a, stage_r, stage_c, stage_d)
+        for lag, stage in zip((0, 1, 0, 2, 3, 4), order):
             if 0 <= t - lag < CHUNKS:
                 stage(t - lag)
 

time: 59.4 us -> 60.8 us (1.024)
  Pallas kernels: 57.7 us -> 59.2 us
    pallas_call x1, Pallas kernels: 49.6 us -> 51 us  [local_fast(): pl.pallas_call(functools.partial(pass_kernel, cap), out_shape=(jax.ShapeD...]
where the time goes in v3:
time: 60.8 us; the launch traced here: 60.6 us
  Pallas kernels  59.2 us (97%)
  local copies, waits for them, and re-layouts  0.8 us (1%)
  between operations  0.65 us (1%)
    pallas_call x1, Pallas kernels, local_fast(): pl.pallas_call(functools.partial(pass_kernel, cap), out_shape=(jax.ShapeD...  51 us
    pallas_call x1, Pallas kernels, local_fast(): pl.pallas_call(down_kernel, grid=(DOWN_STEPS,), in_specs=[pl.BlockSpec((f...  8.12 us

profile of v3, /device:TPU:0, one launch (start us, length us, event | category | flops | bytes accessed | tf_op | source)
XLA Modules:
  0.0 60.6 jit_solution(13929846380934606274)
XLA Ops:
  0.6 51.0 %shard_map.113 = (bf16[64,4096]{1,0:T(8,128)(2,1)}, bf16[1024,256]{1,0:T(8,128)(2,1)}, bf16[256,4096]{1,0:T(8,128)(2,1)}) custom-call(bf16[64,4096]{1,0:T(8,128)(2,1)} %og_hbm.1, f32[2,64]{1,0:T(2,128)} %bitcast.3, s32[2,64]{1,0:T(2,128)} %bitcast.4, s32[2,64]{1,0:T(2,128)} %bitcast.5, s32[1,2]{1,0:T(1,128)} %ct_hbm.1, bf16[1,96,2048]{2,1,0:T(8,128)(2,1)} %sgate_ref.1, ...), custom_call_target="tpu_custom_call" | custom-call | flops 6442450944 | bytes 25165824 | tf_op jit(solution)/shard_map/pallas_call | solution.py:425
  51.7 0.0 copy-start
  51.7 8.1 %shard_map.114 = f32[1024,4096]{1,0:T(8,128)} custom-call(bf16[1024,256]{1,0:T(8,128)(2,1)} %get-tuple-element.6.hid_ref, bf16[256,4096]{1,0:T(8,128)(2,1)} %get-tuple-element.7.rows_ref), custom_call_target="tpu_custom_call" | custom-call | flops 2147483648 | bytes 16777216 | tf_op jit(solution)/shard_map/pallas_call | solution.py:487
  59.8 0.0 copy-done
  59.8 0.8 %copy.13 = bf16[64,4096]{1,0:T(8,128)(2,1)} copy(bf16[64,4096]{1,0:T(8,128)(2,1)S(1)} %copy-done) | data formatting | bytes 1048576
Async XLA Ops:
  51.7 8.1 %copy-start = (bf16[64,4096]{1,0:T(8,128)(2,1)S(1)}, bf16[64,4096]{1,0:T(8,128)(2,1)}, u32[]{:S(2)}) copy-start(bf16[64,4096]{1,0:T(8,128)(2,1)} %get-tuple-element.10) | copy-start | bytes 1572868
